TPU v7x, 256 devices: a whole 4x4x8 slice. The times are simulated.
256 devices in a mesh: replica: 32 (over x, z_hi, core), fsdp: 8 (over y, z_lo).
Axes of the slice: x: 4, y: 4, z: 8 (z_hi: 4, z_lo: 2; z = z_hi * 2 + z_lo), core: 2. Of those that a mesh axis runs over, the one named last changes fastest.
Arguments:
- tokens: bfloat16 [65536, 8192], P(('replica', 'fsdp')), may hold values from -6 to 6
- cotangent: bfloat16 [65536, 512], P(('replica', 'fsdp')), may hold values from -0.125 to 0.125
- gain: float32 [32, 8192], P('replica'), may hold values from 0.1 to 1.9
- value_weight: bfloat16 [32, 8192, 512], P('replica', 'fsdp'), may hold values from -0.25 to 0.25
- fragment: bfloat16 [32, 8192, 1024], P('replica', 'fsdp'), may hold values from -6 to 6
- global_table: float32 [4, 8192, 1024], P(None, ('fsdp', 'replica')), may hold values from -6 to 6
- momentum_table: float32 [4, 8192, 1024], P(None, ('fsdp', 'replica')), may hold values from -4 to 4
- frag_index: int32 [], replicated, may hold values from 0 to 3
Outputs:
- weight_grad: bfloat16 [32, 8192, 512], P('replica', 'fsdp')
- gain_grad: float32 [32, 8192], P('replica')
- new_fragment: bfloat16 [32, 8192, 1024], P('replica', 'fsdp')
- new_global: float32 [4, 8192, 1024], P(None, ('fsdp', 'replica'))
- new_momentum: float32 [4, 8192, 1024], P(None, ('fsdp', 'replica'))
All inputs are finite; a program needn't handle non-finite values.
Results may differ from a plain program's by a relative error of at most 0.017.
Values may be sent and summed in bfloat16 or wider, within the bound.
A program may use at most 128 MiB of HBM per device.

v0:
```python
import jax
import jax.numpy as jnp
from jax import lax
from jax.sharding import PartitionSpec as P

epsilon = 1e-05
outer_rate = 0.7
outer_beta = 0.9
mix_weight = 0.5


def body(tokens, cotangent, gain, value_weight, fragment, global_table, momentum_table, frag_index):
    gains = gain[0]
    weight = value_weight[0]
    floats = tokens.astype(jnp.float32)
    inverse = lax.rsqrt(jnp.mean(floats * floats, axis=-1, keepdims=True) + epsilon)
    normed = floats * inverse
    scaled = (normed * gains).astype(jnp.bfloat16)
    back = lax.dot_general(
        cotangent,
        lax.all_gather(weight, "fsdp", axis=0, tiled=True),
        (((1,), (1,)), ((), ())),
        preferred_element_type=jnp.float32,
    )
    columns = normed
    partial_gain = jnp.sum(columns * back, axis=0)
    gain_grad = lax.psum(partial_gain, "fsdp")
    columns = scaled
    weight_grad = lax.psum_scatter(
        lax.dot_general(
            columns, cotangent, (((0,), (0,)), ((), ())), preferred_element_type=jnp.float32
        ).astype(jnp.bfloat16),
        "fsdp",
        scatter_dimension=0,
        tiled=True,
    )
    chosen = lax.dynamic_index_in_dim(global_table, frag_index, 0, keepdims=False)
    velocity = lax.dynamic_index_in_dim(momentum_table, frag_index, 0, keepdims=False)
    local = fragment[0].astype(jnp.float32)
    replicas = lax.axis_size("replica")
    summed = lax.psum_scatter(
        local.astype(jnp.bfloat16), "replica", scatter_dimension=0, tiled=True
    ).astype(jnp.float32)
    delta = chosen - summed / replicas
    new_velocity = outer_beta * velocity + delta
    new_params = chosen - outer_rate * (delta + outer_beta * new_velocity)
    full_params = lax.all_gather(new_params, "replica", axis=0, tiled=True)
    new_fragment = (mix_weight * local + (1.0 - mix_weight) * full_params).astype(jnp.bfloat16)[
        None
    ]
    new_global = lax.dynamic_update_index_in_dim(global_table, new_params, frag_index, 0)
    new_momentum = lax.dynamic_update_index_in_dim(momentum_table, new_velocity, frag_index, 0)
    return (weight_grad[None], gain_grad[None], new_fragment, new_global, new_momentum)


def solution(mesh):
    placed = (
        P(("replica", "fsdp"), None),
        P(("replica", "fsdp"), None),
        P("replica", None),
        P("replica", "fsdp", None),
        P("replica", "fsdp", None),
        P(None, ("fsdp", "replica"), None),
        P(None, ("fsdp", "replica"), None),
        P(),
    )
    return jax.shard_map(
        body,
        mesh=mesh,
        in_specs=placed,
        out_specs=(
            P("replica", "fsdp", None),
            P("replica", None),
            P("replica", "fsdp", None),
            P(None, ("fsdp", "replica"), None),
            P(None, ("fsdp", "replica"), None),
        ),
        check_vma=False,
    )
```

profile of v0, /device:TPU:2, one launch (start us, length us, event | category | flops | bytes accessed | tf_op | source)
XLA Modules:
  0.0 520.8 jit_solution(3852087064441866261)
XLA Ops:
  7.2 0.0 copy-start
  7.2 0.0 copy-start.5
  7.2 0.0 reduce-scatter.5.cloned.1.call-start
  7.2 1.1 copy.18
  8.3 1.0 copy.19
  9.4 0.0 reduce-scatter.5.cloned.1.call-update
  9.4 0.0 all-gather.4.cloned.1.call-start
  10.1 95.4 %reduce-scatter.5.cloned.1.call-done = bf16[32,1024]{1,0:T(8,128)(2,1)} async-done(((bf16[1024,1024]{1,0:T(8,128)(2,1)}), bf16[32,1024]{1,0:T(8,128)(2,1)}) %reduce-scatter.5.cloned.1.call-update) | async-done | bytes 65552 | tf_op jit(solution)/shard_map/reduce_scatter | solution.py:41
  105.5 1.6 bitcast_subtract_fusion
  107.1 0.0 all-gather.4.cloned.1.call-update
  107.1 0.0 all-gather.6.cloned.1.call-start
  107.1 0.7 all-gather.6.cloned.1.call-update
  107.8 0.0 reduce-scatter.3.cloned.1.call-start
  107.9 3.1 fusion.2
  111.0 0.0 copy-done
  111.0 0.0 copy-done.5
  111.0 8.1 %convolution_convert_fusion = bf16[8192,512]{1,0:T(8,128)(2,1)} fusion(bf16[256,512]{1,0:T(8,128)(2,1)S(1)} %copy-done, bf16[256,8192]{1,0:T(8,128)(2,1)} %param.8, f32[8192]{0:T(1024)S(1)} %bitcast.32, f32[256]{0:T(256)S(1)} %add_rsqrt_fusion), kind=kOutput, calls=%fused_computation | convolution fusion | flops 2160066560 | bytes 12878848 | tf_op jit(solution)/shard_map/dot_general | solution.py:30
  119.1 0.0 copy-start.2
  119.2 0.0 copy-start.1
  119.2 0.0 reduce-scatter.3.cloned.1.call-update
  119.2 0.9 copy-done.2
  120.1 0.9 bitcast_dynamic-update-slice_fusion
  121.0 0.0 copy-start.3
  121.0 0.0 copy-start.4
  121.0 46.4 %all-gather.4.cloned.1.call-done = f32[1024,1024]{1,0:T(8,128)} async-done(((f32[32,1024]{1,0:T(8,128)}), f32[1024,1024]{1,0:T(8,128)}) %all-gather.4.cloned.1.call-update) | async-done | bytes 4194320 | tf_op jit(solution)/shard_map/all_gather | solution.py:47
  167.4 0.0 copy-done.1
  167.4 4.3 fusion.7
  171.7 166.1 %all-gather.6.cloned.1.call-done = bf16[1,8192,512]{2,1,0:T(8,128)(2,1)} async-done(((bf16[1,1024,512]{2,1,0:T(8,128)(2,1)}), bf16[1,8192,512]{2,1,0:T(8,128)(2,1)}) %all-gather.6.cloned.1.call-update) | async-done | bytes 8388624 | tf_op jit(solution)/shard_map/all_gather | solution.py:21
  337.8 7.0 %fusion.8 = f32[8192]{0:T(1024)S(1)} fusion(bf16[256,512]{1,0:T(8,128)(2,1)S(1)} %copy-done, bf16[1,8192,512]{2,1,0:T(8,128)(2,1)} %all-gather.6.cloned.1.call-done, f32[256]{0:T(256)S(1)} %add_rsqrt_fusion, bf16[256,8192]{1,0:T(8,128)(2,1)} %param.8), kind=kOutput, calls=%fused_computation.12 | convolution fusion | flops 2155864064 | bytes 12878848 | tf_op jit(solution)/shard_map/dot_general | solution.py:19
  344.8 0.0 copy-done.3
  344.8 0.0 copy-done.4
  344.8 34.5 %psum.7 = f32[1,8192]{1,0:T(1,128)} all-reduce(f32[1,8192]{1,0:T(1,128)S(1)} %bitcast.30), channel_id=1, replica_groups=mesh['replica'=32,'fsdp'=8] {'fsdp'}, use_global_device_ids=true, to_apply=%region_3.0 | all-reduce | flops 8192 | bytes 65536 | tf_op jit(solution)/shard_map/psum | solution.py:27
  379.2 135.1 %reduce-scatter.3.cloned.1.call-done = bf16[1024,512]{1,0:T(8,128)(2,1)} async-done(((bf16[8192,512]{1,0:T(8,128)(2,1)}), bf16[1024,512]{1,0:T(8,128)(2,1)}) %reduce-scatter.3.cloned.1.call-update) | async-done | bytes 1048592 | tf_op jit(solution)/shard_map/reduce_scatter | solution.py:29
  (1 shorter events, 0.0 us)
Async XLA Ops:
  7.2 103.8 %copy-start = (bf16[256,512]{1,0:T(8,128)(2,1)S(1)}, bf16[256,512]{1,0:T(8,128)(2,1)}, u32[]{:S(2)}) copy-start(bf16[256,512]{1,0:T(8,128)(2,1)} %param.9) | copy-start | bytes 786436
  7.2 103.8 %copy-start.5 = (f32[1,8192]{1,0:T(1,128)S(1)}, f32[1,8192]{1,0:T(1,128)}, u32[]{:S(2)}) copy-start(f32[1,8192]{1,0:T(1,128)} %param.10) | copy-start | bytes 98308
  7.2 98.3 %reduce-scatter.5.cloned.1.call-start = ((), (), s32[]{:S(2)}) async-start(), calls=%async_computation.3 | async-start | bytes 2162688 | tf_op jit(solution)/shard_map/reduce_scatter | solution.py:41
  9.4 158.0 %all-gather.4.cloned.1.call-start = ((), (), s32[]{:S(2)}) async-start(), calls=%async_computation.4 | async-start | bytes 4325376 | tf_op jit(solution)/shard_map/all_gather | solution.py:47
  107.1 230.7 %all-gather.6.cloned.1.call-start = ((), (), s32[]{:S(2)}) async-start(), calls=%async_computation.5 | async-start | bytes 9437184 | tf_op jit(solution)/shard_map/all_gather | solution.py:21
  107.8 406.5 %reduce-scatter.3.cloned.1.call-start = ((), (), s32[]{:S(2)}) async-start(), calls=%async_computation.2 | async-start | bytes 9437184 | tf_op jit(solution)/shard_map/reduce_scatter | solution.py:29
  119.1 0.9 copy-start.2
  119.2 48.2 %copy-start.1 = (bf16[1,1024,1024]{2,1,0:T(8,128)(2,1)S(1)}, bf16[1,1024,1024]{2,1,0:T(8,128)(2,1)}, u32[]{:S(2)}) copy-start(bf16[1,1024,1024]{2,1,0:T(8,128)(2,1)} %param.12) | copy-start | bytes 6291460
  121.0 223.8 %copy-start.3 = (f32[4,32,1024]{2,1,0:T(8,128)}, f32[4,32,1024]{2,1,0:T(8,128)S(1)}, u32[]{:S(2)}) copy-start(f32[4,32,1024]{2,1,0:T(8,128)S(1)} %get-tuple-element.8) | copy-start | bytes 1572868
  121.0 223.8 %copy-start.4 = (f32[4,32,1024]{2,1,0:T(8,128)}, f32[4,32,1024]{2,1,0:T(8,128)S(1)}, u32[]{:S(2)}) copy-start(f32[4,32,1024]{2,1,0:T(8,128)S(1)} %get-tuple-element.7) | copy-start | bytes 1572868
Sparse Core Ops, SparseCore 0:
  11.9 93.5 reduce-scatter.4
  108.6 58.7 all-gather.3
  169.2 168.5 all-gather.5
  340.8 173.4 reduce-scatter.2
where the time goes:
time: 522 us; the launch traced here: 521 us
  waiting for transfers between devices  444 us (85%)
  blocking collectives  34.5 us (7%)
  matrix products  15.1 us (3%)
  between operations  14.5 us (3%)
  other arithmetic  8.97 us (2%)
    all_gather x1, waiting for transfers between devices, body(): lax.all_gather(weight, 'fsdp', axis=0, tiled=True)  166 us
    reduce_scatter x1, waiting for transfers between devices, body(): lax.psum_scatter(lax.dot_general(columns, cotangent, (((0,), (0,)), ((),...  135 us
    reduce_scatter x1, waiting for transfers between devices, body(): lax.psum_scatter(local.astype(jnp.bfloat16), 'replica', scatter_dimension...  95.4 us
    all_gather x1, waiting for transfers between devices, body(): full_params = lax.all_gather(new_params, 'replica', axis=0, tiled=True)  46.4 us
    psum x1, blocking collectives, body(): gain_grad = lax.psum(partial_gain, 'fsdp')  34.5 us
  transfers between devices with their start and end apart: 4, of which 4 were waited for; matrix products, arithmetic and copies ran while one was open for 4% of the time, Pallas kernels for 0%

commit v1 on v0

v1 whole, which is shorter than its diff:
```python
import functools

import jax
import jax.numpy as jnp
from jax import lax
from jax.experimental import pallas as pl
from jax.experimental.pallas import tpu as pltpu
from jax.sharding import PartitionSpec as P

MESH = pl.DeviceIdType.MESH
F32 = jnp.float32
BF16 = jnp.bfloat16

epsilon = 1e-05
outer_rate = 0.7
outer_beta = 0.9
mix_weight = 0.5

NX, NZH, NC = 4, 4, 2
NY, NZL = 4, 2
TOK = 256
D = 8192
BLOCK = 1024
VW = 512
KVW = 1024
ROWS = 32
CHUNKS = 8
WIDTH = BLOCK // CHUNKS
HALVES = 2
HW = KVW // HALVES


def dot_rows(a, b):
    return lax.dot_general(a, b, (((0,), (0,)), ((), ())), preferred_element_type=F32)


def kernel(
    index_ref, tokens, cotangent, gain, weight, fragment, g_table, m_table,
    wg_out, gg_out, nf_out, ng_out, nm_out,
    tok_v, got, cot_v, cots, gain_v, weight_v, zs, zr, wg_v, gg_v,
    frag_v, frag_r, pair_v, xr, quad_v, zhr, params_v, nf_v, gt_v, mt_v, ng_v, nm_v,
    lsem, osem, tok_s, tok_r, cot_s, cot_r, z_s, z_r, gg_s, gg_r,
    fc_s, fc_r, xr_s, xr_r, zh_s, zh_r, az_s, az_r, ax_s, ax_r, ac_s, ac_r,
):
    rep = lax.axis_index("replica")
    fs = lax.axis_index("fsdp")
    x, zh, c = rep // (NZH * NC), (rep // NC) % NZH, rep % NC
    y, zl = fs // NZL, fs % NZL

    def device(dx=0, dzh=0, dc=0, dy=0, dz=0):
        return (
            (((x + dx) % NX) * NZH + (zh + dzh) % NZH) * NC + (c + dc) % NC,
            ((y + dy) % NY) * NZL + (zl + dz) % NZL,
        )

    def remote(src, dst, ssem, rsem, to):
        return pltpu.make_async_remote_copy(
            src_ref=src, dst_ref=dst, send_sem=ssem, recv_sem=rsem,
            device_id=to, device_id_type=MESH,
        )

    local = [
        pltpu.make_async_copy(src, dst, lsem.at[i])
        for i, (src, dst) in enumerate(
            (
                (tokens, tok_v),
                (cotangent, cot_v),
                (fragment, frag_v),
                (weight, weight_v),
                (gain, gain_v),
                (g_table, gt_v),
                (m_table, mt_v),
                (
                    tokens.at[:, pl.ds(pl.multiple_of(y * 2 * BLOCK, 2 * BLOCK), 2 * BLOCK)],
                    got.at[pl.ds(pl.multiple_of(y * TOK, TOK), TOK)],
                ),
            )
        )
    ]
    for i in (2, 0, 1, 7, 3, 4, 5, 6):
        local[i].start()

    partners = (
        [dict(dc=1)]
        + [dict(dx=d) for d in (1, 2, 3)]
        + [dict(dzh=d) for d in (1, 2, 3)]
        + [dict(dy=d) for d in (1, 2, 3)]
        + [dict(dz=1, dy=d) for d in range(4)]
    )
    barrier = pltpu.get_barrier_semaphore()
    for p in partners:
        pl.semaphore_signal(barrier, inc=1, device_id=device(**p), device_id_type=MESH)
    pl.semaphore_wait(barrier, len(partners))

    def half(h):
        return pl.ds(h * HW, HW)

    def core_sum(h):
        return remote(
            fragment.at[:, :, 1 - c, :, half(h)], frag_r.at[:, :, :, half(h)],
            fc_s.at[h], fc_r.at[h], device(dc=1),
        )

    def x_sum(h, d):
        return remote(
            pair_v.at[(x + d) % NX, :, :, half(h)], xr.at[d - 1, :, :, half(h)],
            xr_s.at[h, d - 1], xr_r.at[h, d - 1], device(dx=d),
        )

    def zh_sum(h, d):
        return remote(
            quad_v.at[(zh + d) % NZH, :, half(h)], zhr.at[d - 1, :, half(h)],
            zh_s.at[h, d - 1], zh_r.at[h, d - 1], device(dzh=d),
        )

    def zh_params(h, d):
        part = params_v.at[x, zh, c, :, half(h)]
        return remote(part, part, az_s.at[h, d - 1], az_r.at[h, d - 1], device(dzh=d))

    def x_params(h, d):
        part = params_v.at[x, :, c, :, half(h)]
        return remote(part, part, ax_s.at[h, d - 1], ax_r.at[h, d - 1], device(dx=d))

    def core_params(h):
        part = params_v.at[:, :, c, :, half(h)]
        return remote(part, part, ac_s.at[h], ac_r.at[h], device(dc=1))

    def token_part(k, b, d):
        where = ((y + d) % NY) * 2 * BLOCK + b * BLOCK + k * WIDTH
        return remote(
            tokens.at[:, pl.ds(pl.multiple_of(where, WIDTH), WIDTH)],
            got.at[
                pl.ds(pl.multiple_of(y * TOK, TOK), TOK),
                pl.ds(pl.multiple_of(b * BLOCK + k * WIDTH, WIDTH), WIDTH),
            ],
            tok_s.at[k, b, d - 1], tok_r.at[k, b, d - 1], device(dy=d),
        )

    def cot_part(d):
        part = cots.at[pl.ds(pl.multiple_of(y * TOK, TOK), TOK)]
        return remote(part, part, cot_s.at[d - 1], cot_r.at[d - 1], device(dy=d))

    def z_part(k):
        rows = pl.ds(pl.multiple_of(k * WIDTH, WIDTH), WIDTH)
        return remote(zs.at[rows], zr.at[rows], z_s.at[k], z_r.at[k], device(dz=1))

    def gain_part(i):
        part = gg_v.at[:, pl.ds(pl.multiple_of(fs * BLOCK, BLOCK), BLOCK)]
        return remote(part, part, gg_s.at[i - 1], gg_r.at[i - 1], device(dy=i // 2, dz=i % 2))

    def send_tokens(k):
        for b in (1 - zl, zl):
            for d in (2, 1, 3):
                token_part(k, b, d).start()

    for h in range(HALVES):
        core_sum(h).start()
    send_tokens(0)

    local[2].wait()
    for h in range(HALVES):
        core_sum(h).wait_recv()

        @pl.loop(0, NX * NZH)
        def _(i):
            i, j = i // NZH, i % NZH
            pair_v[i, j, :, half(h)] = (
                frag_v[i, j, c, :, half(h)].astype(F32) + frag_r[i, j, :, half(h)].astype(F32)
            ).astype(BF16)

        for d in (2, 1, 3):
            x_sum(h, d).start()

    local[0].wait()
    local[1].wait()

    @pl.loop(0, TOK // 16)
    def _(i):
        rows = pl.ds(pl.multiple_of(i * 16, 16), 16)
        part = tok_v[rows, :].astype(F32)
        inverse = lax.rsqrt(jnp.sum(part * part, axis=1, keepdims=True) / D + epsilon)
        cots[pl.ds(pl.multiple_of(y * TOK + i * 16, 16), 16), :] = (
            cot_v[rows, :].astype(F32) * inverse
        ).astype(BF16)

    for d in (2, 1, 3):
        cot_part(d).start()
    send_tokens(1)
    send_tokens(2)
    for i in (3, 4, 5, 6, 7):
        local[i].wait()

    def s2(h):
        for d in (1, 3, 2):
            x_sum(h, d).wait_recv()

        @pl.loop(0, NZH)
        def _(j):
            total = pair_v[x, j, :, half(h)].astype(F32)
            for d in (1, 2, 3):
                total = total + xr[d - 1, j, :, half(h)].astype(F32)
            quad_v[j, :, half(h)] = total.astype(BF16)

        for d in (2, 1, 3):
            zh_sum(h, d).start()

    def s3(h):
        for d in (1, 3, 2):
            zh_sum(h, d).wait_recv()
        total = quad_v[zh, :, half(h)].astype(F32)
        for d in (1, 2, 3):
            total = total + zhr[d - 1, :, half(h)].astype(F32)
        picked = index_ref[0]
        chosen = gt_v[picked, :, half(h)]
        velocity = mt_v[picked, :, half(h)]
        delta = chosen - total / (NX * NZH * NC)
        new_velocity = outer_beta * velocity + delta
        new_params = chosen - outer_rate * (delta + outer_beta * new_velocity)
        params_v[x, zh, c, :, half(h)] = new_params.astype(BF16)
        for d in (2, 1, 3):
            zh_params(h, d).start()
        for i in range(4):
            ng_v[i, :, half(h)] = jnp.where(picked == i, new_params, gt_v[i, :, half(h)])
            nm_v[i, :, half(h)] = jnp.where(picked == i, new_velocity, mt_v[i, :, half(h)])
        if h == HALVES - 1:
            pltpu.make_async_copy(ng_v, ng_out, osem.at[2]).start()
            pltpu.make_async_copy(nm_v, nm_out, osem.at[3]).start()

    def s4(h):
        for d in (1, 3, 2):
            zh_params(h, d).wait_recv()
        for d in (2, 1, 3):
            x_params(h, d).start()

    def s5(h):
        for d in (1, 3, 2):
            x_params(h, d).wait_recv()
        core_params(h).start()

    def s6(h):
        core_params(h).wait_recv()

        @pl.loop(0, NX * NZH)
        def _(i):
            i, j = i // NZH, i % NZH
            nf_v[i, j, :, :, half(h)] = (
                mix_weight * frag_v[i, j, :, :, half(h)].astype(F32)
                + (1.0 - mix_weight) * params_v[i, j, :, :, half(h)].astype(F32)
            ).astype(BF16)

        pltpu.make_async_copy(
            nf_v.at[:, :, :, :, half(h)], nf_out.at[:, :, :, :, half(h)], osem.at[h]
        ).start()

    def wg_copy(k):
        rows = pl.ds(pl.multiple_of(k * WIDTH, WIDTH), WIDTH)
        return pltpu.make_async_copy(wg_v.at[rows], wg_out.at[rows], osem.at[4 + k])

    for d in (1, 3, 2):
        cot_part(d).wait_recv()

    steps = {
        0: [(s2, 0)],
        1: [(s2, 1), (s3, 0)],
        2: [(s4, 0), (s3, 1)],
        3: [(s5, 0), (s4, 1)],
        4: [(s6, 0), (s5, 1)],
        5: [(s6, 1)],
    }

    @pl.loop(0, CHUNKS + 1)
    def _(k):
        @pl.when(k < CHUNKS)
        def _():
            for d in (1, 3, 2):
                token_part(k, 1 - zl, d).wait_recv()

            @pl.when(k + 3 < CHUNKS)
            def _():
                send_tokens(k + 3)

            cols = pl.ds(pl.multiple_of((1 - zl) * BLOCK + k * WIDTH, WIDTH), WIDTH)
            zs[pl.ds(pl.multiple_of(k * WIDTH, WIDTH), WIDTH), :] = dot_rows(
                got[:, cols], cots[...]
            ).astype(BF16)
            z_part(k).start()
            for d in (1, 3, 2):
                token_part(k, zl, d).wait_recv()

        @pl.when(k > 0)
        def _():
            j = k - 1
            rows = pl.ds(pl.multiple_of(j * WIDTH, WIDTH), WIDTH)
            cols = pl.ds(pl.multiple_of(zl * BLOCK + j * WIDTH, WIDTH), WIDTH)
            mine = dot_rows(got[:, cols], cots[...])
            z_part(j).wait_recv()
            total = mine + zr[rows, :].astype(F32)
            where = pl.ds(pl.multiple_of(fs * BLOCK + j * WIDTH, WIDTH), WIDTH)
            gains = jnp.broadcast_to(gain_v[:, where], (128, WIDTH)).T
            wg_v[rows, :] = (total * jnp.concatenate([gains] * (VW // 128), axis=1)).astype(BF16)
            wg_copy(j).start()
            terms = total * weight_v[rows, :].astype(F32)
            terms = sum(terms[:, i * 128 : (i + 1) * 128] for i in range(VW // 128))
            gg_v[:, where] = jnp.sum(terms.T, axis=0, keepdims=True)

        for at, calls in steps.items():

            @pl.when(k == at)
            def _():
                for step, h in calls:
                    step(h)

    for i in (7, 3, 5, 4, 6, 2, 1):
        gain_part(i).start()

    for h in range(HALVES):
        core_sum(h).wait_send()
        core_params(h).wait_send()
        for d in (1, 2, 3):
            for part in (x_sum, zh_sum, zh_params, x_params):
                part(h, d).wait_send()
        pltpu.make_async_copy(
            nf_v.at[:, :, :, :, half(h)], nf_out.at[:, :, :, :, half(h)], osem.at[h]
        ).wait()
    pltpu.make_async_copy(ng_v, ng_out, osem.at[2]).wait()
    pltpu.make_async_copy(nm_v, nm_out, osem.at[3]).wait()
    for d in (1, 2, 3):
        cot_part(d).wait_send()

    @pl.loop(0, CHUNKS)
    def _(k):
        for b in (0, 1):
            for d in (1, 2, 3):
                token_part(k, b, d).wait_send()
        z_part(k).wait_send()
        wg_copy(k).wait()

    for i in range(1, 8):
        gain_part(i).wait_recv()
    last = pltpu.make_async_copy(gg_v, gg_out, lsem.at[8])
    last.start()
    for i in range(1, 8):
        gain_part(i).wait_send()
    last.wait()


def body(tokens, cotangent, gain, value_weight, fragment, global_table, momentum_table, frag_index):
    grid = (NX, NZH, NC, ROWS, KVW)
    dma = pltpu.SemaphoreType.DMA
    any_space = pl.BlockSpec(memory_space=pl.ANY)
    wg, gg, nf, ng, nm = pl.pallas_call(
        kernel,
        out_shape=(
            jax.ShapeDtypeStruct((BLOCK, VW), BF16),
            jax.ShapeDtypeStruct((1, D), F32),
            jax.ShapeDtypeStruct(grid, BF16),
            jax.ShapeDtypeStruct((4, ROWS, KVW), F32),
            jax.ShapeDtypeStruct((4, ROWS, KVW), F32),
        ),
        in_specs=[pl.BlockSpec(memory_space=pltpu.SMEM)] + [any_space] * 7,
        out_specs=[any_space] * 5,
        scratch_shapes=[
            pltpu.VMEM((TOK, D), BF16),
            pltpu.VMEM((NY * TOK, 2 * BLOCK), BF16),
            pltpu.VMEM((TOK, VW), BF16),
            pltpu.VMEM((NY * TOK, VW), BF16),
            pltpu.VMEM((1, D), F32),
            pltpu.VMEM((BLOCK, VW), BF16),
            pltpu.VMEM((BLOCK, VW), BF16),
            pltpu.VMEM((BLOCK, VW), BF16),
            pltpu.VMEM((BLOCK, VW), BF16),
            pltpu.VMEM((1, D), F32),
            pltpu.VMEM(grid, BF16),
            pltpu.VMEM((NX, NZH, ROWS, KVW), BF16),
            pltpu.VMEM((NX, NZH, ROWS, KVW), BF16),
            pltpu.VMEM((NX - 1, NZH, ROWS, KVW), BF16),
            pltpu.VMEM((NZH, ROWS, KVW), BF16),
            pltpu.VMEM((NZH - 1, ROWS, KVW), BF16),
            pltpu.VMEM(grid, BF16),
            pltpu.VMEM(grid, BF16),
        ]
        + [pltpu.VMEM((4, ROWS, KVW), F32)] * 4
        + [
            dma((9,)),
            dma((4 + CHUNKS,)),
        ]
        + [dma((CHUNKS, 2, 3))] * 2
        + [dma((3,))] * 2
        + [dma((CHUNKS,))] * 2
        + [dma((7,))] * 2
        + [dma((HALVES,))] * 2
        + [dma((HALVES, 3))] * 8
        + [dma((HALVES,))] * 2,
        compiler_params=pltpu.CompilerParams(
            collective_id=0, has_side_effects=True, vmem_limit_bytes=48 << 20
        ),
        cost_estimate=pl.CostEstimate(
            flops=2 * 2 * TOK * D * VW, bytes_accessed=16 << 20, transcendentals=TOK
        ),
        name="round",
    )(
        frag_index.reshape(1),
        tokens,
        cotangent,
        gain,
        value_weight.reshape(BLOCK, VW),
        fragment.reshape(grid),
        global_table,
        momentum_table,
    )
    return wg[None], gg, nf.reshape(1, BLOCK, KVW), ng, nm


def solution(mesh):
    placed = (
        P(("replica", "fsdp"), None),
        P(("replica", "fsdp"), None),
        P("replica", None),
        P("replica", "fsdp", None),
        P("replica", "fsdp", None),
        P(None, ("fsdp", "replica"), None),
        P(None, ("fsdp", "replica"), None),
        P(),
    )
    return jax.shard_map(
        body,
        mesh=mesh,
        in_specs=placed,
        out_specs=(
            P("replica", "fsdp", None),
            P("replica", None),
            P("replica", "fsdp", None),
            P(None, ("fsdp", "replica"), None),
            P(None, ("fsdp", "replica"), None),
        ),
        check_vma=False,
    )
```

time: 522 us -> 89.9 us (0.17)
  waiting for transfers between devices: 444 us -> 0 us
  Pallas kernels: 0 us -> 78 us
  blocking collectives: 34.5 us -> 0 us
  matrix products: 15.1 us -> 0 us
  between operations: 14.5 us -> 1.31 us
  other arithmetic: 8.97 us -> 0 us
  local copies, waits for them, and re-layouts: 3.95 us -> 9.88 us
    reduce_scatter x2 -> x0, waiting for transfers between devices: 230 us -> none  [the longest x1 135 us: body(): lax.psum_scatter(lax.dot_general(columns, cotangent, (((0,), (0,)), ((),...]
    all_gather x2 -> x0, waiting for transfers between devices: 212 us -> none  [the longest x1 166 us: body(): lax.all_gather(weight, 'fsdp', axis=0, tiled=True)]
    pallas_call x0 -> x1, Pallas kernels: none -> 78 us  [body(): pl.pallas_call(kernel, out_shape=(jax.ShapeDtypeStruct((BLOCK, VW), BF16)...]
    psum x1 -> x0, blocking collectives: 34.5 us -> none  [body(): gain_grad = lax.psum(partial_gain, 'fsdp')]
    dot_general x2 -> x0, matrix products: 15.1 us -> none  [the longest x1 8.14 us: body(): lax.dot_general(columns, cotangent, (((0,), (0,)), ((), ())), preferred_e...]
    unnamed x14 -> x17, local copies, waits for them, and re-layouts: 3.03 us -> 9.88 us
  transfers between devices with their start and end apart: 4 -> 0, of which waited for: 4 -> 0; matrix products, arithmetic and copies ran while one was open for 4% -> 0% of each run, Pallas kernels for 0% -> 0%
where the time goes in v1:
time: 89.9 us; the launch traced here: 89.2 us
  Pallas kernels  78 us (87%)
  local copies, waits for them, and re-layouts  9.88 us (11%)
  between operations  1.31 us (1%)
    pallas_call x1, Pallas kernels, body(): pl.pallas_call(kernel, out_shape=(jax.ShapeDtypeStruct((BLOCK, VW), BF16)...  78 us
    unnamed x17, local copies, waits for them, and re-layouts  9.88 us

profile of v1, /device:TPU:2, one launch (start us, length us, event | category | flops | bytes accessed | tf_op | source)
XLA Modules:
  0.0 89.2 jit_solution(6863226087116085565)
XLA Ops:
  1.3 0.0 copy-start
  1.3 1.2 %copy-done = bf16[1,1024,512]{2,1,0:T(8,128)(2,1)S(1)} copy-done((bf16[1,1024,512]{2,1,0:T(8,128)(2,1)S(1)}, bf16[1,1024,512]{2,1,0:T(8,128)(2,1)}, u32[]{:S(2)}) %copy-start) | copy-done | bytes 1048600
  2.5 0.0 copy-start.1
  2.5 1.0 %copy-done.1 = f32[4,32,1024]{2,1,0:T(8,128)S(1)} copy-done((f32[4,32,1024]{2,1,0:T(8,128)S(1)}, f32[4,32,1024]{2,1,0:T(8,128)}, u32[]{:S(2)}) %copy-start.1) | copy-done | bytes 524312
  3.5 0.0 copy-start.2
  3.6 1.0 %copy-done.2 = f32[4,32,1024]{2,1,0:T(8,128)S(1)} copy-done((f32[4,32,1024]{2,1,0:T(8,128)S(1)}, f32[4,32,1024]{2,1,0:T(8,128)}, u32[]{:S(2)}) %copy-start.2) | copy-done | bytes 524312
  4.6 0.0 copy-start.3
  4.6 0.9 %copy-done.3 = bf16[256,512]{1,0:T(8,128)(2,1)S(1)} copy-done((bf16[256,512]{1,0:T(8,128)(2,1)S(1)}, bf16[256,512]{1,0:T(8,128)(2,1)}, u32[]{:S(2)}) %copy-start.3) | copy-done | bytes 262168
  5.5 0.0 copy-start.4
  5.5 0.8 copy-done.4
  6.3 78.0 %round.1 = (bf16[1024,512]{1,0:T(8,128)(2,1)S(1)}, f32[1,8192]{1,0:T(1,128)S(1)}, bf16[4,4,2,32,1024]{4,3,2,1,0:T(8,128)(2,1)}, f32[4,32,1024]{2,1,0:T(8,128)S(1)}, f32[4,32,1024]{2,1,0:T(8,128)S(1)}) custom-call(s32[1]{0:T(128)} %bitcast.5.index_ref, bf16[256,8192]{1,0:T(8,128)(2,1)} %tokens.1, bf16[256,512]{1,0:T(8,128)(2,1)S(1)} %copy-done.3, ...), custom_call_target="tpu_custom_call" | custom-call | flops 4294967296 | bytes 16777216 | tf_op jit(solution)/shard_map/round/pallas_call | solution.py:351
  84.3 0.0 copy-start.5
  84.3 1.0 %copy.19 = bf16[1,1024,512]{2,1,0:T(8,128)(2,1)} copy(bf16[1,1024,512]{2,1,0:T(8,128)(2,1)S(1)} %bitcast.6) | data formatting | bytes 2097152
  85.3 0.6 copy.20
  85.9 0.4 copy-done.5
  86.3 1.3 %copy.21 = bf16[1,1024,1024]{2,1,0:T(8,128)(2,1)} copy(bf16[1,1024,1024]{2,1,0:T(8,128)(2,1)S(1)} %bitcast.8) | data formatting | bytes 4194304
  87.6 0.8 copy.22
  88.4 0.8 copy.23
Async XLA Ops:
  1.3 1.2 %copy-start = (bf16[1,1024,512]{2,1,0:T(8,128)(2,1)S(1)}, bf16[1,1024,512]{2,1,0:T(8,128)(2,1)}, u32[]{:S(2)}) copy-start(bf16[1,1024,512]{2,1,0:T(8,128)(2,1)} %param.11) | copy-start | bytes 3145732
  2.5 1.0 %copy-start.1 = (f32[4,32,1024]{2,1,0:T(8,128)S(1)}, f32[4,32,1024]{2,1,0:T(8,128)}, u32[]{:S(2)}) copy-start(f32[4,32,1024]{2,1,0:T(8,128)} %g_table.1) | copy-start | bytes 1572868
  3.5 1.0 %copy-start.2 = (f32[4,32,1024]{2,1,0:T(8,128)S(1)}, f32[4,32,1024]{2,1,0:T(8,128)}, u32[]{:S(2)}) copy-start(f32[4,32,1024]{2,1,0:T(8,128)} %m_table.1) | copy-start | bytes 1572868
  4.6 0.9 %copy-start.3 = (bf16[256,512]{1,0:T(8,128)(2,1)S(1)}, bf16[256,512]{1,0:T(8,128)(2,1)}, u32[]{:S(2)}) copy-start(bf16[256,512]{1,0:T(8,128)(2,1)} %cotangent.1) | copy-start | bytes 786436
  5.5 0.8 copy-start.4
  84.3 2.0 %copy-start.5 = (bf16[4,4,2,32,1024]{4,3,2,1,0:T(8,128)(2,1)S(1)}, bf16[4,4,2,32,1024]{4,3,2,1,0:T(8,128)(2,1)}, u32[]{:S(2)}) copy-start(bf16[4,4,2,32,1024]{4,3,2,1,0:T(8,128)(2,1)} %get-tuple-element.12) | copy-start | bytes 6291460

commit v2 on v1

--- a/solution.py
+++ b/solution.py
@@ -26,6 +26,8 @@
 ROWS = 32
 CHUNKS = 8
 WIDTH = BLOCK // CHUNKS
+AHEAD = 4
+LAG = 3
 HALVES = 2
 HW = KVW // HALVES
 
@@ -37,9 +39,9 @@
 def kernel(
     index_ref, tokens, cotangent, gain, weight, fragment, g_table, m_table,
     wg_out, gg_out, nf_out, ng_out, nm_out,
-    tok_v, got, cot_v, cots, gain_v, weight_v, zs, zr, wg_v, gg_v,
+    tok_v, far_v, near_v, part_s, part_v, cot_v, cot_own, cot_near, gain_v, weight_v, zs, zr, wg_v, gg_v,
     frag_v, frag_r, pair_v, xr, quad_v, zhr, params_v, nf_v, gt_v, mt_v, ng_v, nm_v,
-    lsem, osem, tok_s, tok_r, cot_s, cot_r, z_s, z_r, gg_s, gg_r,
+    lsem, osem, far_s, far_r, near_s, near_r, part_ss, part_rs, cot_s, cot_r, z_s, z_r, gg_s, gg_r,
     fc_s, fc_r, xr_s, xr_r, zh_s, zh_r, az_s, az_r, ax_s, ax_r, ac_s, ac_r,
 ):
     rep = lax.axis_index("replica")
@@ -70,14 +72,10 @@
                 (gain, gain_v),
                 (g_table, gt_v),
                 (m_table, mt_v),
-                (
-                    tokens.at[:, pl.ds(pl.multiple_of(y * 2 * BLOCK, 2 * BLOCK), 2 * BLOCK)],
-                    got.at[pl.ds(pl.multiple_of(y * TOK, TOK), TOK)],
-                ),
             )
         )
     ]
-    for i in (2, 0, 1, 7, 3, 4, 5, 6):
+    for i in (2, 0, 1, 3, 4, 5, 6):
         local[i].start()
 
     partners = (
@@ -125,20 +123,45 @@
         part = params_v.at[:, :, c, :, half(h)]
         return remote(part, part, ac_s.at[h], ac_r.at[h], device(dc=1))
 
-    def token_part(k, b, d):
-        where = ((y + d) % NY) * 2 * BLOCK + b * BLOCK + k * WIDTH
-        return remote(
-            tokens.at[:, pl.ds(pl.multiple_of(where, WIDTH), WIDTH)],
-            got.at[
-                pl.ds(pl.multiple_of(y * TOK, TOK), TOK),
-                pl.ds(pl.multiple_of(b * BLOCK + k * WIDTH, WIDTH), WIDTH),
-            ],
-            tok_s.at[k, b, d - 1], tok_r.at[k, b, d - 1], device(dy=d),
-        )
-
-    def cot_part(d):
-        part = cots.at[pl.ds(pl.multiple_of(y * TOK, TOK), TOK)]
-        return remote(part, part, cot_s.at[d - 1], cot_r.at[d - 1], device(dy=d))
+    def at(b, k):
+        return pl.ds(pl.multiple_of(b * BLOCK + k * WIDTH, WIDTH), WIDTH)
+
+    def owned(d, b, k):
+        return pl.ds(
+            pl.multiple_of(((y + d) % NY) * 2 * BLOCK + b * BLOCK + k * WIDTH, WIDTH), WIDTH
+        )
+
+    def side(k):
+        return 1 - 2 * (k % 2)
+
+    def far_part(o, b, k):
+        return remote(
+            tokens.at[:, owned(2, b, k)], far_v.at[:, at(b, k)],
+            far_s.at[o, k], far_r.at[o, k], device(dy=NY - side(k)),
+        )
+
+    def near_part(o, b, k):
+        return remote(
+            tokens.at[:, owned(NY + side(k), b, k)], near_v.at[:, at(b, k)],
+            near_s.at[o, k], near_r.at[o, k], device(dy=NY + side(k)),
+        )
+
+    def product_part(o, b, k):
+        return remote(
+            part_s.at[at(b, k)], part_v.at[at(b, k)],
+            part_ss.at[o, k], part_rs.at[o, k], device(dy=NY - side(k)),
+        )
+
+    def cot_part(i):
+        return remote(
+            cot_own, cot_near.at[1 - i], cot_s.at[i], cot_r.at[1 - i], device(dy=1 + 2 * i)
+        )
+
+    def chunk(q):
+        first, last, odd = 1 - (q + 2 * CHUNKS - 1) // (2 * CHUNKS), (q + 1) // (2 * CHUNKS), q % 2
+        o = (1 - odd) * (1 - first) + last
+        k = odd * ((q + 1) // 2 - last) + (1 - odd) * (q // 2 - 1 + first)
+        return o, o * zl + (1 - o) * (1 - zl), k
 
     def z_part(k):
         rows = pl.ds(pl.multiple_of(k * WIDTH, WIDTH), WIDTH)
@@ -148,14 +171,13 @@
         part = gg_v.at[:, pl.ds(pl.multiple_of(fs * BLOCK, BLOCK), BLOCK)]
         return remote(part, part, gg_s.at[i - 1], gg_r.at[i - 1], device(dy=i // 2, dz=i % 2))
 
-    def send_tokens(k):
-        for b in (1 - zl, zl):
-            for d in (2, 1, 3):
-                token_part(k, b, d).start()
-
     for h in range(HALVES):
         core_sum(h).start()
-    send_tokens(0)
+
+    @pl.loop(0, CHUNKS)
+    def _(q):
+        far_part(*chunk(q)).start()
+
 
     local[2].wait()
     for h in range(HALVES):
@@ -179,15 +201,20 @@
         rows = pl.ds(pl.multiple_of(i * 16, 16), 16)
         part = tok_v[rows, :].astype(F32)
         inverse = lax.rsqrt(jnp.sum(part * part, axis=1, keepdims=True) / D + epsilon)
-        cots[pl.ds(pl.multiple_of(y * TOK + i * 16, 16), 16), :] = (
-            cot_v[rows, :].astype(F32) * inverse
-        ).astype(BF16)
-
-    for d in (2, 1, 3):
-        cot_part(d).start()
-    send_tokens(1)
-    send_tokens(2)
-    for i in (3, 4, 5, 6, 7):
+        cot_own[rows, :] = (cot_v[rows, :].astype(F32) * inverse).astype(BF16)
+
+    for i in (0, 1):
+        cot_part(i).start()
+
+    @pl.loop(CHUNKS, 2 * CHUNKS)
+    def _(q):
+        far_part(*chunk(q)).start()
+
+    @pl.loop(0, AHEAD)
+    def _(q):
+        near_part(*chunk(q)).start()
+
+    for i in (3, 4, 5, 6):
         local[i].wait()
 
     def s2(h):
@@ -256,56 +283,78 @@
         rows = pl.ds(pl.multiple_of(k * WIDTH, WIDTH), WIDTH)
         return pltpu.make_async_copy(wg_v.at[rows], wg_out.at[rows], osem.at[4 + k])
 
-    for d in (1, 3, 2):
-        cot_part(d).wait_recv()
-
-    steps = {
-        0: [(s2, 0)],
-        1: [(s2, 1), (s3, 0)],
-        2: [(s4, 0), (s3, 1)],
-        3: [(s5, 0), (s4, 1)],
-        4: [(s6, 0), (s5, 1)],
-        5: [(s6, 1)],
-    }
-
-    @pl.loop(0, CHUNKS + 1)
-    def _(k):
-        @pl.when(k < CHUNKS)
+    for i in (0, 1):
+        cot_part(1 - i).wait_recv()
+
+    def combine(q):
+        o, b, k = chunk(q)
+        far_part(o, b, k).wait_recv()
+        part_s[at(b, k), :] = (
+            dot_rows(tok_v[:, owned(NY - side(k), b, k)], cot_own[...])
+            + dot_rows(far_v[:, at(b, k)], cot_near[k % 2])
+        ).astype(BF16)
+        product_part(o, b, k).start()
+
+    def collect(o, b, k):
+        near_part(o, b, k).wait_recv()
+        mine = dot_rows(tok_v[:, owned(0, b, k)], cot_own[...]) + dot_rows(
+            near_v[:, at(b, k)], cot_near[1 - k % 2]
+        )
+        product_part(o, b, k).wait_recv()
+        return mine + part_v[at(b, k), :].astype(F32)
+
+    def finish(q):
+        o, _, k = chunk(q)
+        rows = pl.ds(pl.multiple_of(k * WIDTH, WIDTH), WIDTH)
+
+        @pl.when(o == 0)
         def _():
-            for d in (1, 3, 2):
-                token_part(k, 1 - zl, d).wait_recv()
-
-            @pl.when(k + 3 < CHUNKS)
-            def _():
-                send_tokens(k + 3)
-
-            cols = pl.ds(pl.multiple_of((1 - zl) * BLOCK + k * WIDTH, WIDTH), WIDTH)
-            zs[pl.ds(pl.multiple_of(k * WIDTH, WIDTH), WIDTH), :] = dot_rows(
-                got[:, cols], cots[...]
-            ).astype(BF16)
+            zs[rows, :] = collect(o, 1 - zl, k).astype(BF16)
             z_part(k).start()
-            for d in (1, 3, 2):
-                token_part(k, zl, d).wait_recv()
-
-        @pl.when(k > 0)
+
+        @pl.when(o == 1)
         def _():
-            j = k - 1
-            rows = pl.ds(pl.multiple_of(j * WIDTH, WIDTH), WIDTH)
-            cols = pl.ds(pl.multiple_of(zl * BLOCK + j * WIDTH, WIDTH), WIDTH)
-            mine = dot_rows(got[:, cols], cots[...])
-            z_part(j).wait_recv()
+            mine = collect(o, zl, k)
+            z_part(k).wait_recv()
             total = mine + zr[rows, :].astype(F32)
-            where = pl.ds(pl.multiple_of(fs * BLOCK + j * WIDTH, WIDTH), WIDTH)
+            where = pl.ds(pl.multiple_of(fs * BLOCK + k * WIDTH, WIDTH), WIDTH)
             gains = jnp.broadcast_to(gain_v[:, where], (128, WIDTH)).T
             wg_v[rows, :] = (total * jnp.concatenate([gains] * (VW // 128), axis=1)).astype(BF16)
-            wg_copy(j).start()
+            wg_copy(k).start()
             terms = total * weight_v[rows, :].astype(F32)
             terms = sum(terms[:, i * 128 : (i + 1) * 128] for i in range(VW // 128))
             gg_v[:, where] = jnp.sum(terms.T, axis=0, keepdims=True)
 
-        for at, calls in steps.items():
-
-            @pl.when(k == at)
+    steps = {
+        0: [(s2, 0)],
+        2: [(s2, 1)],
+        3: [(s3, 0)],
+        5: [(s3, 1)],
+        6: [(s4, 0)],
+        8: [(s4, 1)],
+        10: [(s5, 0)],
+        12: [(s5, 1)],
+        14: [(s6, 0)],
+        16: [(s6, 1)],
+    }
+
+    @pl.loop(0, 2 * CHUNKS + LAG)
+    def _(q):
+        @pl.when(q < 2 * CHUNKS)
+        def _():
+            combine(q)
+
+            @pl.when(q + AHEAD < 2 * CHUNKS)
+            def _():
+                near_part(*chunk(q + AHEAD)).start()
+
+        @pl.when(q >= LAG)
+        def _():
+            finish(q - LAG)
+
+        for when, calls in steps.items():
+
+            @pl.when(q == when)
             def _():
                 for step, h in calls:
                     step(h)
@@ -324,14 +373,14 @@
         ).wait()
     pltpu.make_async_copy(ng_v, ng_out, osem.at[2]).wait()
     pltpu.make_async_copy(nm_v, nm_out, osem.at[3]).wait()
-    for d in (1, 2, 3):
-        cot_part(d).wait_send()
+    for i in (0, 1):
+        cot_part(i).wait_send()
 
     @pl.loop(0, CHUNKS)
     def _(k):
-        for b in (0, 1):
-            for d in (1, 2, 3):
-                token_part(k, b, d).wait_send()
+        for o in (0, 1):
+            for part in (far_part, near_part, product_part):
+                part(o, o, k).wait_send()
         z_part(k).wait_send()
         wg_copy(k).wait()
 
@@ -344,26 +393,44 @@
     last.wait()
 
 
+def store(*refs):
+    found, out, held, came, went = refs[:5], refs[5:10], refs[10:15], refs[15], refs[16]
+    loads = [pltpu.make_async_copy(found[i], held[i], came.at[i]) for i in range(5)]
+    stores = [pltpu.make_async_copy(held[i], out[i], went.at[i]) for i in range(5)]
+    for i in range(5):
+        loads[i].start()
+    for i in range(5):
+        loads[i].wait()
+        stores[i].start()
+    for i in range(5):
+        stores[i].wait()
+
+
 def body(tokens, cotangent, gain, value_weight, fragment, global_table, momentum_table, frag_index):
     grid = (NX, NZH, NC, ROWS, KVW)
     dma = pltpu.SemaphoreType.DMA
     any_space = pl.BlockSpec(memory_space=pl.ANY)
-    wg, gg, nf, ng, nm = pl.pallas_call(
+    results = (
+        jax.ShapeDtypeStruct((BLOCK, VW), BF16),
+        jax.ShapeDtypeStruct((1, D), F32),
+        jax.ShapeDtypeStruct(grid, BF16),
+        jax.ShapeDtypeStruct((4, ROWS, KVW), F32),
+        jax.ShapeDtypeStruct((4, ROWS, KVW), F32),
+    )
+    found = pl.pallas_call(
         kernel,
-        out_shape=(
-            jax.ShapeDtypeStruct((BLOCK, VW), BF16),
-            jax.ShapeDtypeStruct((1, D), F32),
-            jax.ShapeDtypeStruct(grid, BF16),
-            jax.ShapeDtypeStruct((4, ROWS, KVW), F32),
-            jax.ShapeDtypeStruct((4, ROWS, KVW), F32),
-        ),
+        out_shape=results,
         in_specs=[pl.BlockSpec(memory_space=pltpu.SMEM)] + [any_space] * 7,
         out_specs=[any_space] * 5,
         scratch_shapes=[
             pltpu.VMEM((TOK, D), BF16),
-            pltpu.VMEM((NY * TOK, 2 * BLOCK), BF16),
+            pltpu.VMEM((TOK, 2 * BLOCK), BF16),
+            pltpu.VMEM((TOK, 2 * BLOCK), BF16),
+            pltpu.VMEM((2 * BLOCK, VW), BF16),
+            pltpu.VMEM((2 * BLOCK, VW), BF16),
             pltpu.VMEM((TOK, VW), BF16),
-            pltpu.VMEM((NY * TOK, VW), BF16),
+            pltpu.VMEM((TOK, VW), BF16),
+            pltpu.VMEM((2, TOK, VW), BF16),
             pltpu.VMEM((1, D), F32),
             pltpu.VMEM((BLOCK, VW), BF16),
             pltpu.VMEM((BLOCK, VW), BF16),
@@ -384,15 +451,15 @@
             dma((9,)),
             dma((4 + CHUNKS,)),
         ]
-        + [dma((CHUNKS, 2, 3))] * 2
-        + [dma((3,))] * 2
+        + [dma((2, CHUNKS))] * 6
+        + [dma((2,))] * 2
         + [dma((CHUNKS,))] * 2
         + [dma((7,))] * 2
         + [dma((HALVES,))] * 2
         + [dma((HALVES, 3))] * 8
         + [dma((HALVES,))] * 2,
         compiler_params=pltpu.CompilerParams(
-            collective_id=0, has_side_effects=True, vmem_limit_bytes=48 << 20
+            collective_id=0, has_side_effects=True, vmem_limit_bytes=60 << 20
         ),
         cost_estimate=pl.CostEstimate(
             flops=2 * 2 * TOK * D * VW, bytes_accessed=16 << 20, transcendentals=TOK
@@ -408,6 +475,15 @@
         global_table,
         momentum_table,
     )
+    wg, gg, nf, ng, nm = pl.pallas_call(
+        store,
+        out_shape=results,
+        in_specs=[any_space] * 5,
+        out_specs=[any_space] * 5,
+        scratch_shapes=[pltpu.VMEM(r.shape, r.dtype) for r in results] + [dma((5,))] * 2,
+        compiler_params=pltpu.CompilerParams(vmem_limit_bytes=60 << 20),
+        name="store",
+    )(*found)
     return wg[None], gg, nf.reshape(1, BLOCK, KVW), ng, nm
 
 

time: 89.9 us -> 76.4 us (0.85)
  local copies, waits for them, and re-layouts: 9.88 us -> 0 us
  Pallas kernels: 78 us -> 75.1 us
    unnamed x17 -> x0, local copies, waits for them, and re-layouts: 9.88 us -> none
    pallas_call x1 -> x2, Pallas kernels: 78 us -> 75.1 us  [the longest x1 71.4 us: body(): pl.pallas_call(kernel, out_shape=results, in_specs=[pl.BlockSpec(memory_s...]
where the time goes in v2:
time: 76.4 us; the launch traced here: 76.3 us
  Pallas kernels  75.1 us (98%)
  between operations  1.29 us (2%)
    pallas_call x1, Pallas kernels, body(): pl.pallas_call(kernel, out_shape=results, in_specs=[pl.BlockSpec(memory_s...  71.4 us
    pallas_call x1, Pallas kernels, body(): pl.pallas_call(store, out_shape=results, in_specs=[any_space] * 5, out_sp...  3.68 us

profile of v2, /device:TPU:2, one launch (start us, length us, event | category | flops | bytes accessed | tf_op | source)
XLA Modules:
  0.0 76.3 jit_solution(7013841391571398298)
XLA Ops:
  1.3 71.4 %round.1 = (bf16[1024,512]{1,0:T(8,128)(2,1)}, f32[1,8192]{1,0:T(1,128)}, bf16[4,4,2,32,1024]{4,3,2,1,0:T(8,128)(2,1)}, f32[4,32,1024]{2,1,0:T(8,128)}, f32[4,32,1024]{2,1,0:T(8,128)}) custom-call(s32[1]{0:T(128)} %bitcast.5.index_ref, bf16[256,8192]{1,0:T(8,128)(2,1)} %tokens.1, bf16[256,512]{1,0:T(8,128)(2,1)} %cotangent.1, f32[1,8192]{1,0:T(1,128)} %gain.1, ...), custom_call_target="tpu_custom_call" | custom-call | flops 4294967296 | bytes 16777216 | tf_op jit(solution)/shard_map/round/pallas_call | solution.py:420
  72.7 3.7 %store.1 = (bf16[1024,512]{1,0:T(8,128)(2,1)}, f32[1,8192]{1,0:T(1,128)}, bf16[4,4,2,32,1024]{4,3,2,1,0:T(8,128)(2,1)}, f32[4,32,1024]{2,1,0:T(8,128)}, f32[4,32,1024]{2,1,0:T(8,128)}) custom-call(bf16[1024,512]{1,0:T(8,128)(2,1)} %get-tuple-element.15.refs_0_, f32[1,8192]{1,0:T(1,128)} %get-tuple-element.16.refs_1_, ...), custom_call_target="tpu_custom_call" | custom-call | tf_op jit(solution)/shard_map/store/pallas_call | solution.py:478

commit v3 on v2

--- a/solution.py
+++ b/solution.py
@@ -26,8 +26,8 @@
 ROWS = 32
 CHUNKS = 8
 WIDTH = BLOCK // CHUNKS
-AHEAD = 4
-LAG = 3
+AHEAD = 2
+LAG = 4
 HALVES = 2
 HW = KVW // HALVES
 
@@ -38,10 +38,10 @@
 
 def kernel(
     index_ref, tokens, cotangent, gain, weight, fragment, g_table, m_table,
-    wg_out, gg_out, nf_out, ng_out, nm_out,
-    tok_v, far_v, near_v, part_s, part_v, cot_v, cot_own, cot_near, gain_v, weight_v, zs, zr, wg_v, gg_v,
-    frag_v, frag_r, pair_v, xr, quad_v, zhr, params_v, nf_v, gt_v, mt_v, ng_v, nm_v,
-    lsem, osem, far_s, far_r, near_s, near_r, part_ss, part_rs, cot_s, cot_r, z_s, z_r, gg_s, gg_r,
+    wg_v, gg_v, nf_v, ng_v, nm_v,
+    tok_v, far_v, near_v, part_s, part_v, cot_v, cot_own, cot_near, gain_v, weight_v, zs, zr,
+    frag_v, frag_r, pair_v, xr, quad_v, zhr, params_v, gt_v, mt_v,
+    lsem, far_s, far_r, near_s, near_r, part_ss, part_rs, cot_s, cot_r, z_s, z_r, gg_s, gg_r,
     fc_s, fc_r, xr_s, xr_r, zh_s, zh_r, az_s, az_r, ax_s, ax_r, ac_s, ac_r,
 ):
     rep = lax.axis_index("replica")
@@ -174,10 +174,31 @@
     for h in range(HALVES):
         core_sum(h).start()
 
-    @pl.loop(0, CHUNKS)
+    @pl.loop(0, 8)
     def _(q):
         far_part(*chunk(q)).start()
 
+
+    local[0].wait()
+    local[1].wait()
+
+    @pl.loop(0, TOK // 16)
+    def _(i):
+        rows = pl.ds(pl.multiple_of(i * 16, 16), 16)
+        part = tok_v[rows, :].astype(F32)
+        inverse = lax.rsqrt(jnp.sum(part * part, axis=1, keepdims=True) / D + epsilon)
+        cot_own[rows, :] = (cot_v[rows, :].astype(F32) * inverse).astype(BF16)
+
+    for i in (0, 1):
+        cot_part(i).start()
+
+    @pl.loop(8, 2 * CHUNKS)
+    def _(q):
+        far_part(*chunk(q)).start()
+
+    @pl.loop(0, AHEAD)
+    def _(q):
+        near_part(*chunk(q)).start()
 
     local[2].wait()
     for h in range(HALVES):
@@ -192,27 +213,6 @@
 
         for d in (2, 1, 3):
             x_sum(h, d).start()
-
-    local[0].wait()
-    local[1].wait()
-
-    @pl.loop(0, TOK // 16)
-    def _(i):
-        rows = pl.ds(pl.multiple_of(i * 16, 16), 16)
-        part = tok_v[rows, :].astype(F32)
-        inverse = lax.rsqrt(jnp.sum(part * part, axis=1, keepdims=True) / D + epsilon)
-        cot_own[rows, :] = (cot_v[rows, :].astype(F32) * inverse).astype(BF16)
-
-    for i in (0, 1):
-        cot_part(i).start()
-
-    @pl.loop(CHUNKS, 2 * CHUNKS)
-    def _(q):
-        far_part(*chunk(q)).start()
-
-    @pl.loop(0, AHEAD)
-    def _(q):
-        near_part(*chunk(q)).start()
 
     for i in (3, 4, 5, 6):
         local[i].wait()
@@ -249,9 +249,6 @@
         for i in range(4):
             ng_v[i, :, half(h)] = jnp.where(picked == i, new_params, gt_v[i, :, half(h)])
             nm_v[i, :, half(h)] = jnp.where(picked == i, new_velocity, mt_v[i, :, half(h)])
-        if h == HALVES - 1:
-            pltpu.make_async_copy(ng_v, ng_out, osem.at[2]).start()
-            pltpu.make_async_copy(nm_v, nm_out, osem.at[3]).start()
 
     def s4(h):
         for d in (1, 3, 2):
@@ -274,14 +271,6 @@
                 mix_weight * frag_v[i, j, :, :, half(h)].astype(F32)
                 + (1.0 - mix_weight) * params_v[i, j, :, :, half(h)].astype(F32)
             ).astype(BF16)
-
-        pltpu.make_async_copy(
-            nf_v.at[:, :, :, :, half(h)], nf_out.at[:, :, :, :, half(h)], osem.at[h]
-        ).start()
-
-    def wg_copy(k):
-        rows = pl.ds(pl.multiple_of(k * WIDTH, WIDTH), WIDTH)
-        return pltpu.make_async_copy(wg_v.at[rows], wg_out.at[rows], osem.at[4 + k])
 
     for i in (0, 1):
         cot_part(1 - i).wait_recv()
@@ -318,12 +307,11 @@
             z_part(k).wait_recv()
             total = mine + zr[rows, :].astype(F32)
             where = pl.ds(pl.multiple_of(fs * BLOCK + k * WIDTH, WIDTH), WIDTH)
-            gains = jnp.broadcast_to(gain_v[:, where], (128, WIDTH)).T
-            wg_v[rows, :] = (total * jnp.concatenate([gains] * (VW // 128), axis=1)).astype(BF16)
-            wg_copy(k).start()
             terms = total * weight_v[rows, :].astype(F32)
             terms = sum(terms[:, i * 128 : (i + 1) * 128] for i in range(VW // 128))
             gg_v[:, where] = jnp.sum(terms.T, axis=0, keepdims=True)
+            gains = jnp.broadcast_to(gain_v[:, where], (128, WIDTH)).T
+            wg_v[rows, :] = (total * jnp.concatenate([gains] * (VW // 128), axis=1)).astype(BF16)
 
     steps = {
         0: [(s2, 0)],
@@ -368,11 +356,6 @@
         for d in (1, 2, 3):
             for part in (x_sum, zh_sum, zh_params, x_params):
                 part(h, d).wait_send()
-        pltpu.make_async_copy(
-            nf_v.at[:, :, :, :, half(h)], nf_out.at[:, :, :, :, half(h)], osem.at[h]
-        ).wait()
-    pltpu.make_async_copy(ng_v, ng_out, osem.at[2]).wait()
-    pltpu.make_async_copy(nm_v, nm_out, osem.at[3]).wait()
     for i in (0, 1):
         cot_part(i).wait_send()
 
@@ -382,28 +365,19 @@
             for part in (far_part, near_part, product_part):
                 part(o, o, k).wait_send()
         z_part(k).wait_send()
-        wg_copy(k).wait()
 
     for i in range(1, 8):
         gain_part(i).wait_recv()
-    last = pltpu.make_async_copy(gg_v, gg_out, lsem.at[8])
-    last.start()
     for i in range(1, 8):
         gain_part(i).wait_send()
-    last.wait()
 
 
 def store(*refs):
-    found, out, held, came, went = refs[:5], refs[5:10], refs[10:15], refs[15], refs[16]
-    loads = [pltpu.make_async_copy(found[i], held[i], came.at[i]) for i in range(5)]
-    stores = [pltpu.make_async_copy(held[i], out[i], went.at[i]) for i in range(5)]
-    for i in range(5):
-        loads[i].start()
-    for i in range(5):
-        loads[i].wait()
-        stores[i].start()
-    for i in range(5):
-        stores[i].wait()
+    copies = [pltpu.make_async_copy(refs[i], refs[5 + i], refs[10].at[i]) for i in range(5)]
+    for copy in copies:
+        copy.start()
+    for copy in copies:
+        copy.wait()
 
 
 def body(tokens, cotangent, gain, value_weight, fragment, global_table, momentum_table, frag_index):
@@ -419,9 +393,9 @@
     )
     found = pl.pallas_call(
         kernel,
-        out_shape=results,
+        out_shape=[pltpu.VMEM(r.shape, r.dtype) for r in results],
         in_specs=[pl.BlockSpec(memory_space=pltpu.SMEM)] + [any_space] * 7,
-        out_specs=[any_space] * 5,
+        out_specs=[pl.BlockSpec(memory_space=pltpu.VMEM)] * 5,
         scratch_shapes=[
             pltpu.VMEM((TOK, D), BF16),
             pltpu.VMEM((TOK, 2 * BLOCK), BF16),
@@ -435,8 +409,6 @@
             pltpu.VMEM((BLOCK, VW), BF16),
             pltpu.VMEM((BLOCK, VW), BF16),
             pltpu.VMEM((BLOCK, VW), BF16),
-            pltpu.VMEM((BLOCK, VW), BF16),
-            pltpu.VMEM((1, D), F32),
             pltpu.VMEM(grid, BF16),
             pltpu.VMEM((NX, NZH, ROWS, KVW), BF16),
             pltpu.VMEM((NX, NZH, ROWS, KVW), BF16),
@@ -444,13 +416,9 @@
             pltpu.VMEM((NZH, ROWS, KVW), BF16),
             pltpu.VMEM((NZH - 1, ROWS, KVW), BF16),
             pltpu.VMEM(grid, BF16),
-            pltpu.VMEM(grid, BF16),
         ]
-        + [pltpu.VMEM((4, ROWS, KVW), F32)] * 4
-        + [
-            dma((9,)),
-            dma((4 + CHUNKS,)),
-        ]
+        + [pltpu.VMEM((4, ROWS, KVW), F32)] * 2
+        + [dma((7,))]
         + [dma((2, CHUNKS))] * 6
         + [dma((2,))] * 2
         + [dma((CHUNKS,))] * 2
@@ -459,7 +427,7 @@
         + [dma((HALVES, 3))] * 8
         + [dma((HALVES,))] * 2,
         compiler_params=pltpu.CompilerParams(
-            collective_id=0, has_side_effects=True, vmem_limit_bytes=60 << 20
+            collective_id=0, has_side_effects=True, vmem_limit_bytes=56 << 20
         ),
         cost_estimate=pl.CostEstimate(
             flops=2 * 2 * TOK * D * VW, bytes_accessed=16 << 20, transcendentals=TOK
@@ -480,8 +448,8 @@
         out_shape=results,
         in_specs=[any_space] * 5,
         out_specs=[any_space] * 5,
-        scratch_shapes=[pltpu.VMEM(r.shape, r.dtype) for r in results] + [dma((5,))] * 2,
-        compiler_params=pltpu.CompilerParams(vmem_limit_bytes=60 << 20),
+        scratch_shapes=[dma((5,))],
+        compiler_params=pltpu.CompilerParams(vmem_limit_bytes=4 << 20),
         name="store",
     )(*found)
     return wg[None], gg, nf.reshape(1, BLOCK, KVW), ng, nm

time: 76.4 us -> 72.3 us (0.946)
  Pallas kernels: 75.1 us -> 70.9 us
    pallas_call x1, Pallas kernels: 71.4 us -> 68.8 us  [body(): pl.pallas_call(kernel, out_shape=[pltpu.VMEM(r.shape, r.dtype) for r in r...]
    pallas_call x1, Pallas kernels: 3.68 us -> 2.06 us  [body(): pl.pallas_call(store, out_shape=results, in_specs=[any_space] * 5, out_sp...]
where the time goes in v3:
time: 72.3 us; the launch traced here: 72.2 us
  Pallas kernels  70.9 us (98%)
  between operations  1.29 us (2%)
    pallas_call x1, Pallas kernels, body(): pl.pallas_call(kernel, out_shape=[pltpu.VMEM(r.shape, r.dtype) for r in r...  68.8 us
    pallas_call x1, Pallas kernels, body(): pl.pallas_call(store, out_shape=results, in_specs=[any_space] * 5, out_sp...  2.06 us

profile of v3, /device:TPU:2, one launch (start us, length us, event | category | flops | bytes accessed | tf_op | source)
XLA Modules:
  0.0 72.2 jit_solution(16304927038398955270)
XLA Ops:
  1.3 68.8 %round.1 = (bf16[1024,512]{1,0:T(8,128)(2,1)S(1)}, f32[1,8192]{1,0:T(1,128)S(1)}, bf16[4,4,2,32,1024]{4,3,2,1,0:T(8,128)(2,1)S(1)}, f32[4,32,1024]{2,1,0:T(8,128)S(1)}, f32[4,32,1024]{2,1,0:T(8,128)S(1)}) custom-call(s32[1]{0:T(128)} %bitcast.5.index_ref, bf16[256,8192]{1,0:T(8,128)(2,1)} %tokens.1, bf16[256,512]{1,0:T(8,128)(2,1)} %cotangent.1, ...), custom_call_target="tpu_custom_call" | custom-call | flops 4294967296 | bytes 16777216 | tf_op jit(solution)/shard_map/round/pallas_call | solution.py:394
  70.1 2.1 %store.1 = (bf16[1024,512]{1,0:T(8,128)(2,1)}, f32[1,8192]{1,0:T(1,128)}, bf16[4,4,2,32,1024]{4,3,2,1,0:T(8,128)(2,1)}, f32[4,32,1024]{2,1,0:T(8,128)}, f32[4,32,1024]{2,1,0:T(8,128)}) custom-call(bf16[1024,512]{1,0:T(8,128)(2,1)S(1)} %get-tuple-element.15.refs_0_, f32[1,8192]{1,0:T(1,128)S(1)} %get-tuple-element.16.refs_1_, ...), custom_call_target="tpu_custom_call" | custom-call | tf_op jit(solution)/shard_map/store/pallas_call | solution.py:446

commit v4 on v3

--- a/solution.py
+++ b/solution.py
@@ -26,9 +26,11 @@
 ROWS = 32
 CHUNKS = 8
 WIDTH = BLOCK // CHUNKS
+SPLIT = 6
+DOWN = CHUNKS - SPLIT
 AHEAD = 2
 LAG = 4
-HALVES = 2
+HALVES = 4
 HW = KVW // HALVES
 
 
@@ -39,9 +41,11 @@
 def kernel(
     index_ref, tokens, cotangent, gain, weight, fragment, g_table, m_table,
     wg_v, gg_v, nf_v, ng_v, nm_v,
-    tok_v, far_v, near_v, part_s, part_v, cot_v, cot_own, cot_near, gain_v, weight_v, zs, zr,
+    tok_v, far_v, near_v, part_s, part_v, cot_v, cot_own, cot_near, gain_v,
+    swap_v, cot_swap, away_s, away_v, side_s, side_v, sum_s, sum_v, weight_v, zs, zr,
     frag_v, frag_r, pair_v, xr, quad_v, zhr, params_v, gt_v, mt_v,
     lsem, far_s, far_r, near_s, near_r, part_ss, part_rs, cot_s, cot_r, z_s, z_r, gg_s, gg_r,
+    swap_ss, swap_rs, cs_s, cs_r, away_ss, away_rs, side_ss, side_rs, sum_ss, sum_rs,
     fc_s, fc_r, xr_s, xr_r, zh_s, zh_r, az_s, az_r, ax_s, ax_r, ac_s, ac_r,
 ):
     rep = lax.axis_index("replica")
@@ -78,17 +82,37 @@
     for i in (2, 0, 1, 3, 4, 5, 6):
         local[i].start()
 
-    partners = (
+    near_partners = (
         [dict(dc=1)]
         + [dict(dx=d) for d in (1, 2, 3)]
-        + [dict(dzh=d) for d in (1, 2, 3)]
         + [dict(dy=d) for d in (1, 2, 3)]
         + [dict(dz=1, dy=d) for d in range(4)]
     )
     barrier = pltpu.get_barrier_semaphore()
-    for p in partners:
-        pl.semaphore_signal(barrier, inc=1, device_id=device(**p), device_id_type=MESH)
-    pl.semaphore_wait(barrier, len(partners))
+
+    def greet(to):
+        pl.semaphore_signal(barrier, inc=1, device_id=to, device_id_type=MESH)
+
+    for p in near_partners:
+        greet(device(**p))
+
+    @pl.when(zh >= 2)
+    def _():
+        greet(device(dzh=NZH + 5 - 2 * zh))
+        pl.semaphore_wait(barrier, len(near_partners) + 3)
+        greet(device(dzh=NZH - zh))
+        greet(device(dzh=NZH + 1 - zh))
+
+    @pl.when(zh < 2)
+    def _():
+        pl.semaphore_wait(barrier, len(near_partners) + zh)
+        for d in (1, 2, 3):
+            greet(device(dzh=d))
+
+    def later_barrier():
+        @pl.when(zh < 2)
+        def _():
+            pl.semaphore_wait(barrier, 3 - zh)
 
     def half(h):
         return pl.ds(h * HW, HW)
@@ -124,7 +148,8 @@
         return remote(part, part, ac_s.at[h], ac_r.at[h], device(dc=1))
 
     def at(b, k):
-        return pl.ds(pl.multiple_of(b * BLOCK + k * WIDTH, WIDTH), WIDTH)
+        start = b * BLOCK + k * WIDTH
+        return pl.ds(start if isinstance(start, int) else pl.multiple_of(start, WIDTH), WIDTH)
 
     def owned(d, b, k):
         return pl.ds(
@@ -157,8 +182,36 @@
             cot_own, cot_near.at[1 - i], cot_s.at[i], cot_r.at[1 - i], device(dy=1 + 2 * i)
         )
 
+    def swap_part(i, d):
+        col = pl.multiple_of(d * 2 * BLOCK + (1 - zl) * BLOCK + (SPLIT + i) * WIDTH, WIDTH)
+        return remote(
+            tokens.at[:, pl.ds(col, WIDTH)], swap_v.at[i, d],
+            swap_ss.at[i, d], swap_rs.at[i, d], device(dz=1),
+        )
+
+    def cot_swap_part():
+        return remote(cot_own, cot_swap, cs_s, cs_r, device(dz=1))
+
+    def away_part(i):
+        return remote(
+            away_s.at[i], away_v.at[i], away_ss.at[i], away_rs.at[i],
+            device(dy=NY - side(SPLIT + i)),
+        )
+
+    def side_part(i):
+        return remote(
+            side_s.at[i], side_v.at[i], side_ss.at[i], side_rs.at[i],
+            device(dy=NY + side(SPLIT + i)),
+        )
+
+    def sum_part(i):
+        return remote(
+            sum_s.at[i], sum_v.at[i], sum_ss.at[i], sum_rs.at[i],
+            device(dy=NY - side(SPLIT + i)),
+        )
+
     def chunk(q):
-        first, last, odd = 1 - (q + 2 * CHUNKS - 1) // (2 * CHUNKS), (q + 1) // (2 * CHUNKS), q % 2
+        first, last, odd = 1 - (q + 2 * SPLIT - 1) // (2 * SPLIT), (q + 1) // (2 * SPLIT), q % 2
         o = (1 - odd) * (1 - first) + last
         k = odd * ((q + 1) // 2 - last) + (1 - odd) * (q // 2 - 1 + first)
         return o, o * zl + (1 - o) * (1 - zl), k
@@ -174,9 +227,13 @@
     for h in range(HALVES):
         core_sum(h).start()
 
-    @pl.loop(0, 8)
+    @pl.loop(0, SPLIT)
     def _(q):
         far_part(*chunk(q)).start()
+
+    for i in range(DOWN):
+        for d in range(NY):
+            swap_part(i, d).start()
 
 
     local[0].wait()
@@ -191,8 +248,9 @@
 
     for i in (0, 1):
         cot_part(i).start()
-
-    @pl.loop(8, 2 * CHUNKS)
+    cot_swap_part().start()
+
+    @pl.loop(SPLIT, 2 * SPLIT)
     def _(q):
         far_part(*chunk(q)).start()
 
@@ -228,6 +286,8 @@
                 total = total + xr[d - 1, j, :, half(h)].astype(F32)
             quad_v[j, :, half(h)] = total.astype(BF16)
 
+        if h == 0:
+            later_barrier()
         for d in (2, 1, 3):
             zh_sum(h, d).start()
 
@@ -292,6 +352,15 @@
         product_part(o, b, k).wait_recv()
         return mine + part_v[at(b, k), :].astype(F32)
 
+    def conclude(k, total):
+        rows = at(0, k)
+        where = pl.ds(pl.multiple_of(fs * BLOCK + k * WIDTH, WIDTH), WIDTH)
+        terms = total * weight_v[rows, :].astype(F32)
+        terms = sum(terms[:, i * 128 : (i + 1) * 128] for i in range(VW // 128))
+        gg_v[:, where] = jnp.sum(terms.T, axis=0, keepdims=True)
+        gains = jnp.broadcast_to(gain_v[:, where], (128, WIDTH)).T
+        wg_v[rows, :] = (total * jnp.concatenate([gains] * (VW // 128), axis=1)).astype(BF16)
+
     def finish(q):
         o, _, k = chunk(q)
         rows = pl.ds(pl.multiple_of(k * WIDTH, WIDTH), WIDTH)
@@ -305,34 +374,64 @@
         def _():
             mine = collect(o, zl, k)
             z_part(k).wait_recv()
-            total = mine + zr[rows, :].astype(F32)
-            where = pl.ds(pl.multiple_of(fs * BLOCK + k * WIDTH, WIDTH), WIDTH)
-            terms = total * weight_v[rows, :].astype(F32)
-            terms = sum(terms[:, i * 128 : (i + 1) * 128] for i in range(VW // 128))
-            gg_v[:, where] = jnp.sum(terms.T, axis=0, keepdims=True)
-            gains = jnp.broadcast_to(gain_v[:, where], (128, WIDTH)).T
-            wg_v[rows, :] = (total * jnp.concatenate([gains] * (VW // 128), axis=1)).astype(BF16)
+            conclude(k, mine + zr[rows, :].astype(F32))
+
+    def both(i, d):
+        if i == 0 and d == 2:
+            cot_swap_part().wait_recv()
+        if d == 2:
+            for e in range(NY):
+                swap_part(i, e).wait_recv()
+        return dot_rows(tok_v[:, owned(d, zl, SPLIT + i)], cot_own[...]) + dot_rows(
+            swap_v[i, (y + d) % NY], cot_swap[...]
+        )
+
+    def away(i):
+        away_s[i] = both(i, 2).astype(BF16)
+        away_part(i).start()
+
+    def beside(i):
+        side_s[i] = both(i, NY + side(SPLIT + i)).astype(BF16)
+        side_part(i).start()
+
+    def pass_on(i):
+        mine = both(i, NY - side(SPLIT + i))
+        away_part(i).wait_recv()
+        sum_s[i] = (mine + away_v[i].astype(F32)).astype(BF16)
+        sum_part(i).start()
+
+    def add_up(i):
+        mine = both(i, 0)
+        side_part(i).wait_recv()
+        sum_part(i).wait_recv()
+        conclude(SPLIT + i, mine + side_v[i].astype(F32) + sum_v[i].astype(F32))
 
     steps = {
-        0: [(s2, 0)],
-        2: [(s2, 1)],
-        3: [(s3, 0)],
-        5: [(s3, 1)],
-        6: [(s4, 0)],
-        8: [(s4, 1)],
-        10: [(s5, 0)],
-        12: [(s5, 1)],
-        14: [(s6, 0)],
-        16: [(s6, 1)],
+        0: [(away, 0)],
+        1: [(s2, 0), (away, 1)],
+        2: [(s2, 1), (beside, 0)],
+        3: [(s3, 0), (s2, 2), (beside, 1)],
+        4: [(s3, 1), (s2, 3), (pass_on, 0)],
+        5: [(s3, 2), (pass_on, 1)],
+        6: [(s4, 0), (s3, 3)],
+        7: [(s4, 1), (add_up, 0)],
+        8: [(s4, 2), (add_up, 1)],
+        9: [(s5, 0), (s4, 3)],
+        10: [(s5, 1)],
+        11: [(s5, 2)],
+        12: [(s6, 0), (s5, 3)],
+        13: [(s6, 1)],
+        14: [(s6, 2)],
+        15: [(s6, 3)],
     }
 
-    @pl.loop(0, 2 * CHUNKS + LAG)
+    @pl.loop(0, 2 * SPLIT + LAG)
     def _(q):
-        @pl.when(q < 2 * CHUNKS)
+        @pl.when(q < 2 * SPLIT)
         def _():
             combine(q)
 
-            @pl.when(q + AHEAD < 2 * CHUNKS)
+            @pl.when(q + AHEAD < 2 * SPLIT)
             def _():
                 near_part(*chunk(q + AHEAD)).start()
 
@@ -359,7 +458,14 @@
     for i in (0, 1):
         cot_part(i).wait_send()
 
-    @pl.loop(0, CHUNKS)
+    cot_swap_part().wait_send()
+    for i in range(DOWN):
+        for d in range(NY):
+            swap_part(i, d).wait_send()
+        for part in (away_part, side_part, sum_part):
+            part(i).wait_send()
+
+    @pl.loop(0, SPLIT)
     def _(k):
         for o in (0, 1):
             for part in (far_part, near_part, product_part):
@@ -406,6 +512,11 @@
             pltpu.VMEM((TOK, VW), BF16),
             pltpu.VMEM((2, TOK, VW), BF16),
             pltpu.VMEM((1, D), F32),
+            pltpu.VMEM((DOWN, NY, TOK, WIDTH), BF16),
+            pltpu.VMEM((TOK, VW), BF16),
+        ]
+        + [pltpu.VMEM((DOWN, WIDTH, VW), BF16)] * 6
+        + [
             pltpu.VMEM((BLOCK, VW), BF16),
             pltpu.VMEM((BLOCK, VW), BF16),
             pltpu.VMEM((BLOCK, VW), BF16),
@@ -423,6 +534,9 @@
         + [dma((2,))] * 2
         + [dma((CHUNKS,))] * 2
         + [dma((7,))] * 2
+        + [dma((DOWN, NY))] * 2
+        + [dma] * 2
+        + [dma((DOWN,))] * 6
         + [dma((HALVES,))] * 2
         + [dma((HALVES, 3))] * 8
         + [dma((HALVES,))] * 2,

time: 72.3 us -> 70.9 us (0.981)
  Pallas kernels: 70.9 us -> 69.5 us
    pallas_call x1, Pallas kernels: 68.8 us -> 67.5 us  [body(): pl.pallas_call(kernel, out_shape=[pltpu.VMEM(r.shape, r.dtype) for r in r...]
where the time goes in v4:
time: 70.9 us; the launch traced here: 70.8 us
  Pallas kernels  69.5 us (98%)
  between operations  1.29 us (2%)
    pallas_call x1, Pallas kernels, body(): pl.pallas_call(kernel, out_shape=[pltpu.VMEM(r.shape, r.dtype) for r in r...  67.5 us
    pallas_call x1, Pallas kernels, body(): pl.pallas_call(store, out_shape=results, in_specs=[any_space] * 5, out_sp...  2.06 us

profile of v4, /device:TPU:2, one launch (start us, length us, event | category | flops | bytes accessed | tf_op | source)
XLA Modules:
  0.0 70.8 jit_solution(9810937668006072582)
XLA Ops:
  1.3 67.5 %round.1 = (bf16[1024,512]{1,0:T(8,128)(2,1)S(1)}, f32[1,8192]{1,0:T(1,128)S(1)}, bf16[4,4,2,32,1024]{4,3,2,1,0:T(8,128)(2,1)S(1)}, f32[4,32,1024]{2,1,0:T(8,128)S(1)}, f32[4,32,1024]{2,1,0:T(8,128)S(1)}) custom-call(s32[1]{0:T(128)} %bitcast.5.index_ref, bf16[256,8192]{1,0:T(8,128)(2,1)} %tokens.1, bf16[256,512]{1,0:T(8,128)(2,1)} %cotangent.1, ...), custom_call_target="tpu_custom_call" | custom-call | flops 4294967296 | bytes 16777216 | tf_op jit(solution)/shard_map/round/pallas_call | solution.py:500
  68.7 2.1 %store.1 = (bf16[1024,512]{1,0:T(8,128)(2,1)}, f32[1,8192]{1,0:T(1,128)}, bf16[4,4,2,32,1024]{4,3,2,1,0:T(8,128)(2,1)}, f32[4,32,1024]{2,1,0:T(8,128)}, f32[4,32,1024]{2,1,0:T(8,128)}) custom-call(bf16[1024,512]{1,0:T(8,128)(2,1)S(1)} %get-tuple-element.15.refs_0_, f32[1,8192]{1,0:T(1,128)S(1)} %get-tuple-element.16.refs_1_, ...), custom_call_target="tpu_custom_call" | custom-call | tf_op jit(solution)/shard_map/store/pallas_call | solution.py:560

commit v5 on v4

--- a/solution.py
+++ b/solution.py
@@ -28,7 +28,7 @@
 WIDTH = BLOCK // CHUNKS
 SPLIT = 6
 DOWN = CHUNKS - SPLIT
-AHEAD = 2
+AHEAD = 3
 LAG = 4
 HALVES = 4
 HW = KVW // HALVES
@@ -79,8 +79,6 @@
             )
         )
     ]
-    for i in (2, 0, 1, 3, 4, 5, 6):
-        local[i].start()
 
     near_partners = (
         [dict(dc=1)]
@@ -96,6 +94,9 @@
     for p in near_partners:
         greet(device(**p))
 
+    for i in (0, 1, 2, 3, 4, 5, 6):
+        local[i].start()
+
     @pl.when(zh >= 2)
     def _():
         greet(device(dzh=NZH + 5 - 2 * zh))
@@ -156,25 +157,28 @@
             pl.multiple_of(((y + d) % NY) * 2 * BLOCK + b * BLOCK + k * WIDTH, WIDTH), WIDTH
         )
 
-    def side(k):
-        return 1 - 2 * (k % 2)
+    def turn(o, k):
+        return (1 - o) * ((k + SPLIT - 1) // SPLIT) + o * ((k + 1) // SPLIT)
+
+    def side(o, k):
+        return 1 - 2 * turn(o, k)
 
     def far_part(o, b, k):
         return remote(
             tokens.at[:, owned(2, b, k)], far_v.at[:, at(b, k)],
-            far_s.at[o, k], far_r.at[o, k], device(dy=NY - side(k)),
+            far_s.at[o, k], far_r.at[o, k], device(dy=NY - side(o, k)),
         )
 
     def near_part(o, b, k):
         return remote(
-            tokens.at[:, owned(NY + side(k), b, k)], near_v.at[:, at(b, k)],
-            near_s.at[o, k], near_r.at[o, k], device(dy=NY + side(k)),
+            tokens.at[:, owned(NY + side(o, k), b, k)], near_v.at[:, at(b, k)],
+            near_s.at[o, k], near_r.at[o, k], device(dy=NY + side(o, k)),
         )
 
     def product_part(o, b, k):
         return remote(
             part_s.at[at(b, k)], part_v.at[at(b, k)],
-            part_ss.at[o, k], part_rs.at[o, k], device(dy=NY - side(k)),
+            part_ss.at[o, k], part_rs.at[o, k], device(dy=NY - side(o, k)),
         )
 
     def cot_part(i):
@@ -195,19 +199,19 @@
     def away_part(i):
         return remote(
             away_s.at[i], away_v.at[i], away_ss.at[i], away_rs.at[i],
-            device(dy=NY - side(SPLIT + i)),
+            device(dy=NY - 1 + 2 * (i % 2)),
         )
 
     def side_part(i):
         return remote(
             side_s.at[i], side_v.at[i], side_ss.at[i], side_rs.at[i],
-            device(dy=NY + side(SPLIT + i)),
+            device(dy=NY + 1 - 2 * (i % 2)),
         )
 
     def sum_part(i):
         return remote(
             sum_s.at[i], sum_v.at[i], sum_ss.at[i], sum_rs.at[i],
-            device(dy=NY - side(SPLIT + i)),
+            device(dy=NY - 1 + 2 * (i % 2)),
         )
 
     def chunk(q):
@@ -224,13 +228,13 @@
         part = gg_v.at[:, pl.ds(pl.multiple_of(fs * BLOCK, BLOCK), BLOCK)]
         return remote(part, part, gg_s.at[i - 1], gg_r.at[i - 1], device(dy=i // 2, dz=i % 2))
 
-    for h in range(HALVES):
-        core_sum(h).start()
 
     @pl.loop(0, SPLIT)
     def _(q):
         far_part(*chunk(q)).start()
 
+    for h in range(HALVES):
+        core_sum(h).start()
     for i in range(DOWN):
         for d in range(NY):
             swap_part(i, d).start()
@@ -323,6 +327,12 @@
 
     def s6(h):
         core_params(h).wait_recv()
+        core_sum(h).wait_send()
+        for d in (1, 2, 3):
+            for part in (x_sum, zh_sum, zh_params, x_params):
+                part(h, d).wait_send()
+        if h > 0:
+            core_params(h - 1).wait_send()
 
         @pl.loop(0, NX * NZH)
         def _(i):
@@ -339,15 +349,15 @@
         o, b, k = chunk(q)
         far_part(o, b, k).wait_recv()
         part_s[at(b, k), :] = (
-            dot_rows(tok_v[:, owned(NY - side(k), b, k)], cot_own[...])
-            + dot_rows(far_v[:, at(b, k)], cot_near[k % 2])
+            dot_rows(tok_v[:, owned(NY - side(o, k), b, k)], cot_own[...])
+            + dot_rows(far_v[:, at(b, k)], cot_near[turn(o, k)])
         ).astype(BF16)
         product_part(o, b, k).start()
 
     def collect(o, b, k):
         near_part(o, b, k).wait_recv()
         mine = dot_rows(tok_v[:, owned(0, b, k)], cot_own[...]) + dot_rows(
-            near_v[:, at(b, k)], cot_near[1 - k % 2]
+            near_v[:, at(b, k)], cot_near[1 - turn(o, k)]
         )
         product_part(o, b, k).wait_recv()
         return mine + part_v[at(b, k), :].astype(F32)
@@ -361,6 +371,11 @@
         gains = jnp.broadcast_to(gain_v[:, where], (128, WIDTH)).T
         wg_v[rows, :] = (total * jnp.concatenate([gains] * (VW // 128), axis=1)).astype(BF16)
 
+    def sent(q):
+        o, b, k = chunk(q)
+        for part in (far_part, near_part, product_part):
+            part(o, b, k).wait_send()
+
     def finish(q):
         o, _, k = chunk(q)
         rows = pl.ds(pl.multiple_of(k * WIDTH, WIDTH), WIDTH)
@@ -391,38 +406,45 @@
         away_part(i).start()
 
     def beside(i):
-        side_s[i] = both(i, NY + side(SPLIT + i)).astype(BF16)
+        side_s[i] = both(i, NY + 1 - 2 * (i % 2)).astype(BF16)
         side_part(i).start()
 
     def pass_on(i):
-        mine = both(i, NY - side(SPLIT + i))
+        mine = both(i, NY - 1 + 2 * (i % 2))
         away_part(i).wait_recv()
         sum_s[i] = (mine + away_v[i].astype(F32)).astype(BF16)
         sum_part(i).start()
 
     def add_up(i):
+        if i == 0:
+            for j in (0, 1):
+                cot_part(j).wait_send()
+            cot_swap_part().wait_send()
+        for d in range(NY):
+            swap_part(i, d).wait_send()
+        for part in (away_part, side_part):
+            part(i).wait_send()
         mine = both(i, 0)
         side_part(i).wait_recv()
         sum_part(i).wait_recv()
         conclude(SPLIT + i, mine + side_v[i].astype(F32) + sum_v[i].astype(F32))
 
     steps = {
-        0: [(away, 0)],
-        1: [(s2, 0), (away, 1)],
-        2: [(s2, 1), (beside, 0)],
-        3: [(s3, 0), (s2, 2), (beside, 1)],
-        4: [(s3, 1), (s2, 3), (pass_on, 0)],
-        5: [(s3, 2), (pass_on, 1)],
-        6: [(s4, 0), (s3, 3)],
-        7: [(s4, 1), (add_up, 0)],
-        8: [(s4, 2), (add_up, 1)],
-        9: [(s5, 0), (s4, 3)],
-        10: [(s5, 1)],
-        11: [(s5, 2)],
-        12: [(s6, 0), (s5, 3)],
-        13: [(s6, 1)],
-        14: [(s6, 2)],
-        15: [(s6, 3)],
+        1: [(s2, 0)],
+        2: [(away, 0), (s2, 1)],
+        3: [(s2, 2)],
+        4: [(s3, 0), (away, 1), (s2, 3)],
+        5: [(s3, 1), (beside, 0)],
+        6: [(s3, 2), (pass_on, 0)],
+        7: [(s4, 0), (s3, 3), (beside, 1)],
+        8: [(s4, 1), (pass_on, 1)],
+        9: [(s4, 2)],
+        10: [(s4, 3), (add_up, 0)],
+        11: [(s5, 0), (s5, 1), (add_up, 1)],
+        12: [(s5, 2)],
+        13: [(s5, 3)],
+        14: [(s6, 0), (s6, 1)],
+        15: [(s6, 2), (s6, 3)],
     }
 
     @pl.loop(0, 2 * SPLIT + LAG)
@@ -435,10 +457,6 @@
             def _():
                 near_part(*chunk(q + AHEAD)).start()
 
-        @pl.when(q >= LAG)
-        def _():
-            finish(q - LAG)
-
         for when, calls in steps.items():
 
             @pl.when(q == when)
@@ -446,30 +464,26 @@
                 for step, h in calls:
                     step(h)
 
+        @pl.when(q >= LAG)
+        def _():
+            finish(q - LAG)
+
+        @pl.when((q >= LAG) & (q < 2 * SPLIT))
+        def _():
+            sent(q - LAG)
+
     for i in (7, 3, 5, 4, 6, 2, 1):
         gain_part(i).start()
 
-    for h in range(HALVES):
-        core_sum(h).wait_send()
-        core_params(h).wait_send()
-        for d in (1, 2, 3):
-            for part in (x_sum, zh_sum, zh_params, x_params):
-                part(h, d).wait_send()
-    for i in (0, 1):
-        cot_part(i).wait_send()
-
-    cot_swap_part().wait_send()
+    core_params(HALVES - 1).wait_send()
     for i in range(DOWN):
-        for d in range(NY):
-            swap_part(i, d).wait_send()
-        for part in (away_part, side_part, sum_part):
-            part(i).wait_send()
-
-    @pl.loop(0, SPLIT)
-    def _(k):
-        for o in (0, 1):
-            for part in (far_part, near_part, product_part):
-                part(o, o, k).wait_send()
+        sum_part(i).wait_send()
+
+    @pl.loop(2 * SPLIT - LAG, 2 * SPLIT)
+    def _(q):
+        sent(q)
+
+    for k in range(SPLIT):
         z_part(k).wait_send()
 
     for i in range(1, 8):

time: 70.9 us -> 67.7 us (0.955)
  Pallas kernels: 69.5 us -> 66.3 us
    pallas_call x1, Pallas kernels: 67.5 us -> 64.3 us  [body(): pl.pallas_call(kernel, out_shape=[pltpu.VMEM(r.shape, r.dtype) for r in r...]
where the time goes in v5:
time: 67.7 us; the launch traced here: 67.6 us
  Pallas kernels  66.3 us (98%)
  between operations  1.29 us (2%)
    pallas_call x1, Pallas kernels, body(): pl.pallas_call(kernel, out_shape=[pltpu.VMEM(r.shape, r.dtype) for r in r...  64.3 us
    pallas_call x1, Pallas kernels, body(): pl.pallas_call(store, out_shape=results, in_specs=[any_space] * 5, out_sp...  2.06 us

profile of v5, /device:TPU:2, one launch (start us, length us, event | category | flops | bytes accessed | tf_op | source)
XLA Modules:
  0.0 67.6 jit_solution(6078516555014382616)
XLA Ops:
  1.3 64.3 %round.1 = (bf16[1024,512]{1,0:T(8,128)(2,1)S(1)}, f32[1,8192]{1,0:T(1,128)S(1)}, bf16[4,4,2,32,1024]{4,3,2,1,0:T(8,128)(2,1)S(1)}, f32[4,32,1024]{2,1,0:T(8,128)S(1)}, f32[4,32,1024]{2,1,0:T(8,128)S(1)}) custom-call(s32[1]{0:T(128)} %bitcast.5.index_ref, bf16[256,8192]{1,0:T(8,128)(2,1)} %tokens.1, bf16[256,512]{1,0:T(8,128)(2,1)} %cotangent.1, ...), custom_call_target="tpu_custom_call" | custom-call | flops 4294967296 | bytes 16777216 | tf_op jit(solution)/shard_map/round/pallas_call | solution.py:514
  65.6 2.1 %store.1 = (bf16[1024,512]{1,0:T(8,128)(2,1)}, f32[1,8192]{1,0:T(1,128)}, bf16[4,4,2,32,1024]{4,3,2,1,0:T(8,128)(2,1)}, f32[4,32,1024]{2,1,0:T(8,128)}, f32[4,32,1024]{2,1,0:T(8,128)}) custom-call(bf16[1024,512]{1,0:T(8,128)(2,1)S(1)} %get-tuple-element.15.refs_0_, f32[1,8192]{1,0:T(1,128)S(1)} %get-tuple-element.16.refs_1_, ...), custom_call_target="tpu_custom_call" | custom-call | tf_op jit(solution)/shard_map/store/pallas_call | solution.py:574

commit v6 on v5

--- a/solution.py
+++ b/solution.py
@@ -444,7 +444,6 @@
         12: [(s5, 2)],
         13: [(s5, 3)],
         14: [(s6, 0), (s6, 1)],
-        15: [(s6, 2), (s6, 3)],
     }
 
     @pl.loop(0, 2 * SPLIT + LAG)
@@ -474,6 +473,8 @@
 
     for i in (7, 3, 5, 4, 6, 2, 1):
         gain_part(i).start()
+    for h in range(2, HALVES):
+        s6(h)
 
     core_params(HALVES - 1).wait_send()
     for i in range(DOWN):

time: 67.7 us -> 67.7 us (level)
  no operation moved by 1% of the time
where the time goes in v6:
time: 67.7 us; the launch traced here: 67.6 us
  Pallas kernels  66.3 us (98%)
  between operations  1.29 us (2%)
    pallas_call x1, Pallas kernels, body(): pl.pallas_call(kernel, out_shape=[pltpu.VMEM(r.shape, r.dtype) for r in r...  64.3 us
    pallas_call x1, Pallas kernels, body(): pl.pallas_call(store, out_shape=results, in_specs=[any_space] * 5, out_sp...  2.06 us

profile of v6, /device:TPU:2, one launch (start us, length us, event | category | flops | bytes accessed | tf_op | source)
XLA Modules:
  0.0 67.6 jit_solution(11272034401138147898)
XLA Ops:
  1.3 64.3 %round.1 = (bf16[1024,512]{1,0:T(8,128)(2,1)S(1)}, f32[1,8192]{1,0:T(1,128)S(1)}, bf16[4,4,2,32,1024]{4,3,2,1,0:T(8,128)(2,1)S(1)}, f32[4,32,1024]{2,1,0:T(8,128)S(1)}, f32[4,32,1024]{2,1,0:T(8,128)S(1)}) custom-call(s32[1]{0:T(128)} %bitcast.5.index_ref, bf16[256,8192]{1,0:T(8,128)(2,1)} %tokens.1, bf16[256,512]{1,0:T(8,128)(2,1)} %cotangent.1, ...), custom_call_target="tpu_custom_call" | custom-call | flops 4294967296 | bytes 16777216 | tf_op jit(solution)/shard_map/round/pallas_call | solution.py:515
  65.6 2.1 %store.1 = (bf16[1024,512]{1,0:T(8,128)(2,1)}, f32[1,8192]{1,0:T(1,128)}, bf16[4,4,2,32,1024]{4,3,2,1,0:T(8,128)(2,1)}, f32[4,32,1024]{2,1,0:T(8,128)}, f32[4,32,1024]{2,1,0:T(8,128)}) custom-call(bf16[1024,512]{1,0:T(8,128)(2,1)S(1)} %get-tuple-element.15.refs_0_, f32[1,8192]{1,0:T(1,128)S(1)} %get-tuple-element.16.refs_1_, ...), custom_call_target="tpu_custom_call" | custom-call | tf_op jit(solution)/shard_map/store/pallas_call | solution.py:575
